TPU v7x, 32 devices: a whole 2x2x4 slice. The times are simulated.
32 devices in a mesh: mem: 8 (over z, x), lev: 4 (over y, core).
Axes of the slice: x: 2, y: 2, z: 4, core: 2. Of those that a mesh axis runs over, the one named last changes fastest.
Arguments:
- background_trajectories: float32 [1024, 8, 8, 128], P('mem', None, 'lev')
- linear_sensor_mapping: float32 [8, 128, 128], P('lev'), may hold values from -0.1875 to 0.1875
- jittered_sensor_values: float32 [1024, 8, 128], P('mem'), may hold values from -6 to 6
- residual_precision_tiles: float32 [8, 128, 128], replicated, as said below
- measurement_tile_table: int32 [8, 16], replicated, may hold values from 0 to 7, as said below
- holder_rank: int32 [8], replicated, may hold values from 0 to 7, as said below
Outputs:
- analysis: float32 [1024, 16, 8, 128], P(None, 'mem', 'lev')
Inputs may be any that keep to these rules, and one draw needn't show every extreme that they name: `measurement_tile_table`: entry (b, q) lies within 12 blocks of b on the cycle of blocks; a row's entries are distinct where 8 >= 25. `holder_rank`: each index owns at most 2 blocks, and some index owns exactly 2. `residual_precision_tiles`: symmetric.
All inputs are finite; a program needn't handle non-finite values.
Results may differ from a plain program's by a relative error of at most 0.0094.
Values may be sent and summed in bfloat16 or wider, within the bound.
A program may use at most 128 MiB of HBM per device.

v0:
```python
import jax
import jax.numpy as jnp
from jax import lax
from jax.sharding import PartitionSpec as P

REACH = 12
CAP = 2


def shards(
    background_trajectories,
    linear_sensor_mapping,
    jittered_sensor_values,
    residual_precision_tiles,
    measurement_tile_table,
    holder_rank,
):
    largest_ordering_label = lax.Precision.HIGHEST
    mem_count = lax.axis_size("mem")
    my_index = lax.axis_index("mem")
    resident_realizations, tile_count, layer_count, mesh_sites = background_trajectories.shape
    obs_width = linear_sensor_mapping.shape[2]
    listed = measurement_tile_table.shape[1]
    capacity = CAP
    slot_count = mem_count * capacity
    partial_observed = jnp.einsum(
        "vhsg,sgl->vhl",
        background_trajectories,
        linear_sensor_mapping,
        precision=largest_ordering_label,
    )
    aggregated_total = lax.psum(partial_observed, "lev")
    departure = jittered_sensor_values - aggregated_total
    weighted = jnp.einsum(
        "mbo,bop->mbp", departure, residual_precision_tiles, precision=largest_ordering_label
    ).astype(jnp.bfloat16)
    background_values_mapped = aggregated_total.astype(jnp.bfloat16)
    blocks = jnp.arange(tile_count, dtype=jnp.int32)
    shared_owner = holder_rank[:, None] == holder_rank[None, :]
    earlier = blocks[None, :] < blocks[:, None]
    order_rank = jnp.sum((shared_owner & earlier).astype(jnp.int32), axis=1)
    slot_of_block = holder_rank * capacity + order_rank
    slot_ids = jnp.arange(slot_count, dtype=jnp.int32)
    matches = slot_of_block[None, :] == slot_ids[:, None]
    active_slot = jnp.any(matches, axis=1)
    tile_at_place = jnp.sum(jnp.where(matches, blocks[None, :], 0), axis=1)
    obs_index = jnp.take(measurement_tile_table, tile_at_place, axis=0)
    offsets_abs = jnp.abs(tile_at_place[:, None] - obs_index)
    cycle_gap = jnp.minimum(offsets_abs, tile_count - offsets_abs).astype(jnp.float32)
    scaled_gap = 2.0 * cycle_gap / REACH
    taper_weight = 1.0 / (1.0 + scaled_gap * scaled_gap)
    outgoing = (
        jnp.take(background_trajectories, tile_at_place, axis=1)
        * active_slot.astype(jnp.float32)[None, :, None, None]
    )
    outgoing = outgoing.reshape(
        resident_realizations, mem_count, capacity, layer_count * mesh_sites
    )
    states = lax.all_to_all(outgoing, "mem", split_axis=1, concat_axis=0, tiled=True).reshape(
        -1, capacity, layer_count * mesh_sites
    )
    total_members = states.shape[0]
    gathered = (
        lax.all_gather(background_values_mapped, "mem", axis=0, tiled=True),
        lax.all_gather(weighted, "mem", axis=0, tiled=True),
    )
    mine_index = lax.dynamic_slice_in_dim(obs_index, my_index * capacity, capacity, 0).reshape(-1)
    mine_live = lax.dynamic_slice_in_dim(active_slot, my_index * capacity, capacity, 0)
    mine_mask = jnp.repeat(mine_live, listed).astype(jnp.bfloat16)
    pred_rows = jnp.take(gathered[0], mine_index, axis=1) * mine_mask[None, :, None]
    weight_rows = jnp.take(gathered[1], mine_index, axis=1) * mine_mask[None, :, None]
    my_taper = lax.dynamic_slice_in_dim(taper_weight, my_index * capacity, capacity, 0)
    state_half = states.astype(jnp.bfloat16)
    mean_pred = jnp.mean(pred_rows, axis=0, dtype=jnp.float32)
    pred_pert = (
        (pred_rows - mean_pred)
        .astype(jnp.bfloat16)
        .reshape(total_members, capacity, listed * obs_width)
    )
    weight_cols = weight_rows.reshape(total_members, capacity, listed * obs_width)
    covariance = jnp.einsum(
        "mcx,mcy->cxy", state_half, pred_pert, preferred_element_type=jnp.float32
    )
    column_scale = jnp.repeat(my_taper, obs_width, axis=1) / (total_members - 1)
    covariance = (covariance * column_scale[:, None, :]).astype(jnp.bfloat16)
    increment = jnp.einsum(
        "mcy,cxy->mcx", weight_cols, covariance, preferred_element_type=jnp.float32
    )
    return (states + increment).reshape(total_members, capacity, layer_count, mesh_sites)


def solution(mesh):
    in_specs = (
        P("mem", None, "lev", None),
        P("lev", None, None),
        P("mem", None, None),
        P(),
        P(),
        P(),
    )
    out_specs = P(None, "mem", "lev", None)
    return jax.shard_map(shards, mesh=mesh, in_specs=in_specs, out_specs=out_specs, check_vma=False)
```

profile of v0, /device:TPU:0, one launch (start us, length us, event | category | flops | bytes accessed | tf_op | source)
XLA Modules:
  0.0 226.8 jit_solution(5101924670259297547)
XLA Ops:
  6.5 3.2 %convolution_bitcast_fusion = f32[128,8,128]{2,0,1:T(8,128)} fusion(f32[128,8,2,128]{3,2,1,0:T(2,128)} %param.8, f32[2,128,128]{2,1,0:T(8,128)} %param.9), kind=kOutput, calls=%fused_computation.12 | convolution fusion | flops 402653184 | bytes 1703936 | tf_op jit(solution)/shard_map/vhsg,sgl->vhl/dot_general | solution.py:26
  9.8 36.0 %all-reduce.2.cloned.1.call-done = f32[128,8,128]{2,0,1:T(8,128)} async-done(((f32[128,8,128]{2,0,1:T(8,128)}), f32[128,8,128]{2,0,1:T(8,128)}) %all-reduce.2.cloned.1.call-update) | async-done | bytes 524304 | tf_op jit(solution)/shard_map/psum | solution.py:32
  45.8 1.8 convert_element_type.53
  47.6 0.9 convert_reduce_fusion.1
  48.6 0.7 multiply_add_fusion
  49.2 0.1 select_reduce_fusion
  49.3 0.1 reduce_sum.33
  49.4 5.8 %gather_fusion = f32[16,128,2,128]{3,2,1,0:T(2,128)} fusion(f32[128,8,2,128]{3,2,1,0:T(2,128)} %param.8, s32[1024]{0:T(1024)S(1)} %pad_clamp_fusion.1), kind=kCustom, calls=%fused_computation.2 | custom fusion | bytes 4194368 | tf_op jit(solution)/shard_map/jit(_take)/gather | solution.py:53
  55.3 2.8 %copy.31 = f32[128,16,2,128]{0,3,2,1:T(8,128)S(1)} copy(f32[128,16,2,128]{3,2,0,1:T(2,128)} %bitcast.46) | data formatting | bytes 4194304 | tf_op jit(solution)/shard_map/jit(_take)/gather | solution.py:53
  58.0 0.1 fusion.6
  58.1 0.1 reshape.78
  58.2 1.6 select_multiply_fusion
  59.8 5.5 %all-to-all-start = ((f32[128,8,2,256]{0,3,2,1:T(8,128)}), f32[128,8,2,256]{0,3,2,1:T(8,128)S(1)}, u32[]{:S(2)}, u32[]{:S(2)}) async-start(f32[128,8,2,256]{0,3,2,1:T(8,128)} %select_multiply_fusion), calls=%async_computation | async-start | bytes 4194304 | tf_op jit(solution)/shard_map/all_to_all | solution.py:59
  65.4 2.4 %fusion.1 = bf16[128,8,128]{2,0,1:T(8,128)(2,1)} fusion(f32[8,128,128]{2,1,0:T(8,128)S(1)} %copy-done, f32[128,8,128]{2,0,1:T(8,128)S(1)} %copy-done.2, f32[128,8,128]{2,1,0:T(8,128)} %param.10), kind=kOutput, calls=%fused_computation.14 | convolution fusion | flops 201588736 | bytes 1835008 | tf_op jit(solution)/shard_map/mbo,bop->mbp/dot_general | solution.py:34
  67.9 0.6 gather_fusion.1
  68.5 0.1 broadcast_subtract_fusion
  68.6 0.1 reshape.74
  68.7 0.1 dynamic-slice_convert_fusion
  68.8 0.1 convert_element_type.55
  69.1 62.4 %all-to-all-done = f32[128,8,2,256]{0,3,2,1:T(8,128)S(1)} async-done(((f32[128,8,2,256]{0,3,2,1:T(8,128)}), f32[128,8,2,256]{0,3,2,1:T(8,128)S(1)}, u32[]{:S(2)}, u32[]{:S(2)}) %all-to-all-start) | async-done | bytes 2097184 | tf_op jit(solution)/shard_map/all_to_all | solution.py:59
  131.5 2.5 %copy.32 = f32[8,128,1,2,256]{1,0,4,3,2:T(8,128)} copy(f32[8,128,1,2,256]{1,4,3,0,2:T(8,128)S(1)} %bitcast.44) | data formatting | bytes 4194304 | tf_op jit(solution)/shard_map/all_to_all | solution.py:59
  134.0 1.7 reshape.73
  135.8 6.7 %gather_fusion.2 = bf16[32,1024,128]{2,1,0:T(8,128)(2,1)} fusion(bf16[1024,8,128]{2,0,1:T(8,128)(2,1)} %all-gather.3.cloned.1.call-done, s32[1024]{0:T(1024)S(1)} %pad_clamp_fusion), kind=kCustom, calls=%fused_computation.clone | custom fusion | bytes 16777344 | tf_op jit(solution)/shard_map/jit(_take)/gather | solution.py:70
  142.5 7.5 %convert_reduce_fusion = f32[32,128]{1,0:T(8,128)S(1)} fusion(bf16[32]{0:T(256)(128)(2,1)S(1)} %convert_element_type.55, bf16[32,1024,128]{2,1,0:T(8,128)(2,1)} %gather_fusion.2, pred[32]{0:T(512)(128)(4,1)S(1)} %compare_and_fusion.1), kind=kLoop, calls=%fused_computation.5 | loop fusion | flops 16773120 | bytes 8405088 | tf_op jit(solution)/shard_map/reduce_sum | solution.py:74
  150.0 11.0 %fusion = bf16[1024,32,128]{2,0,1:T(8,128)(2,1)} fusion(f32[32,128]{1,0:T(8,128)S(1)} %broadcast_multiply_fusion, bf16[32]{0:T(256)(128)(2,1)S(1)} %convert_element_type.55, bf16[32,1024,128]{2,1,0:T(8,128)(2,1)} %gather_fusion.2, pred[32]{0:T(512)(128)(4,1)S(1)} %compare_and_fusion.1), kind=kLoop, calls=%fused_computation.6 | loop fusion | flops 20971520 | bytes 16793696 | tf_op jit(solution)/shard_map/convert_element_type | solution.py:77
  161.0 11.9 %copy.34 = bf16[1024,32,128]{0,2,1:T(8,128)(2,1)} copy(bf16[1024,32,128]{2,0,1:T(8,128)(2,1)} %fusion) | data formatting | bytes 16777216 | tf_op jit(solution)/shard_map/convert_element_type | solution.py:77
  173.0 5.5 %all-gather.5.cloned.1.call-done = bf16[1024,8,128]{2,0,1:T(8,128)(2,1)} async-done(((bf16[128,8,128]{2,0,1:T(8,128)(2,1)}), bf16[1024,8,128]{2,0,1:T(8,128)(2,1)}) %all-gather.5.cloned.1.call-update) | async-done | bytes 2097168 | tf_op jit(solution)/shard_map/all_gather | solution.py:65
  178.4 6.6 %gather_fusion.3 = bf16[32,1024,128]{2,1,0:T(8,128)(2,1)} fusion(bf16[1024,8,128]{2,0,1:T(8,128)(2,1)} %all-gather.5.cloned.1.call-done, s32[1024]{0:T(1024)S(1)} %pad_clamp_fusion), kind=kCustom, calls=%fused_computation.1.clone | custom fusion | bytes 16777344 | tf_op jit(solution)/shard_map/jit(_take)/gather | solution.py:71
  185.0 7.4 %bitcast_multiply_fusion = bf16[1024,32,128]{2,0,1:T(8,128)(2,1)} fusion(bf16[32,1024,128]{2,1,0:T(8,128)(2,1)} %gather_fusion.3, pred[32]{0:T(512)(128)(4,1)S(1)} %compare_and_fusion.1, bf16[32]{0:T(256)(128)(2,1)S(1)} %convert_element_type.55), kind=kLoop, calls=%fused_computation.7 | loop fusion | flops 8388608 | bytes 16777312 | tf_op jit(solution)/shard_map/mul | solution.py:71
  192.5 11.9 %copy.37 = bf16[1024,32,128]{0,2,1:T(8,128)(2,1)} copy(bf16[1024,32,128]{2,0,1:T(8,128)(2,1)} %bitcast_multiply_fusion) | data formatting | bytes 16777216 | tf_op jit(solution)/shard_map/mul | solution.py:71
  204.4 11.7 %bitcast_add_fusion = f32[1024,2,256]{0,2,1:T(8,128)} fusion(f32[1024,2,256]{0,2,1:T(8,128)S(1)} %reshape.73, bf16[1024,2,2048]{0,2,1:T(8,128)(2,1)} %bitcast.43, bf16[1024,2,2048]{0,2,1:T(8,128)(2,1)} %bitcast.42, f32[2,2048]{1,0:T(2,128)S(1)} %bitcast.48), kind=kOutput, calls=%fused_computation.10 | convolution fusion | flops 4298113024 | bytes 20987904 | tf_op jit(solution)/shard_map/mcy,cxy->mcx/dot_general | solution.py:86
  216.1 4.1 %copy.39 = f32[1024,2,2,128]{3,2,1,0:T(2,128)} copy(f32[1024,2,2,128]{0,3,2,1:T(8,128)} %bitcast.47) | data formatting | bytes 4194304 | tf_op jit(solution)/shard_map/reshape | solution.py:89
  (29 shorter events, 0.4 us)
Async XLA Ops:
  6.5 58.9 %copy-start = (f32[8,128,128]{2,1,0:T(8,128)S(1)}, f32[8,128,128]{2,1,0:T(8,128)}, u32[]{:S(2)}) copy-start(f32[8,128,128]{2,1,0:T(8,128)} %param.11) | copy-start | bytes 1572868
  6.5 39.3 %all-reduce.2.cloned.1.call-start = ((), (), s32[]{:S(2)}) async-start(), calls=%async_computation.1 | async-start | bytes 1048576 | tf_op jit(solution)/shard_map/psum | solution.py:32
  9.8 126.0 %all-gather.3.cloned.1.call-start = ((), (), s32[]{:S(2)}) async-start(), calls=%async_computation.2 | async-start | bytes 2359296 | tf_op jit(solution)/shard_map/all_gather | solution.py:64
  49.4 16.0 %copy-start.2 = (f32[128,8,128]{2,0,1:T(8,128)S(1)}, f32[128,8,128]{2,0,1:T(8,128)}, u32[]{:S(2)}) copy-start(f32[128,8,128]{2,0,1:T(8,128)} %all-reduce.2.cloned.1.call-done) | copy-start | bytes 1572868
  55.3 12.7 %copy-start.3 = (s32[8,16]{1,0:T(8,128)S(1)}, s32[8,16]{1,0:T(8,128)}, u32[]{:S(2)}) copy-start(s32[8,16]{1,0:T(8,128)} %param.12) | copy-start | bytes 1540
  59.8 71.7 %all-to-all-start = ((f32[128,8,2,256]{0,3,2,1:T(8,128)}), f32[128,8,2,256]{0,3,2,1:T(8,128)S(1)}, u32[]{:S(2)}, u32[]{:S(2)}) async-start(f32[128,8,2,256]{0,3,2,1:T(8,128)} %select_multiply_fusion), calls=%async_computation | async-start | bytes 4194304 | tf_op jit(solution)/shard_map/all_to_all | solution.py:59
  65.4 113.1 %all-gather.5.cloned.1.call-start = ((), (), s32[]{:S(2)}) async-start(), calls=%async_computation.3 | async-start | bytes 2359296 | tf_op jit(solution)/shard_map/all_gather | solution.py:65
  204.4 15.8 %copy-start.1 = (f32[8,128,128]{2,1,0:T(8,128)S(1)}, f32[8,128,128]{2,1,0:T(8,128)}, u32[]{:S(2)}) copy-start(f32[8,128,128]{2,1,0:T(8,128)} %param.11) | copy-start | bytes 1572868
Sparse Core Ops, SparseCore 0:
  9.9 35.8 all-reduce.1
  48.0 81.7 all-gather.2
  132.0 46.3 all-gather.4
where the time goes:
time: 228 us; the launch traced here: 227 us
  waiting for transfers between devices  104 us (46%)
  local copies, waits for them, and re-layouts  55.2 us (24%)
  other arithmetic  31.3 us (14%)
  matrix products  17.4 us (8%)
  between operations  13.3 us (6%)
  starting transfers between devices  5.62 us (2%)
    all_to_all x1, waiting for transfers between devices, shards(): lax.all_to_all(outgoing, 'mem', split_axis=1, concat_axis=0, tiled=True)  62.4 us
    psum x1, waiting for transfers between devices, shards(): aggregated_total = lax.psum(partial_observed, 'lev')  36 us
    convert_element_type x1, local copies, waits for them, and re-layouts, shards(): pred_pert = (pred_rows - mean_pred).astype(jnp.bfloat16).reshape(total_me...  11.9 us
    mul x1, local copies, waits for them, and re-layouts, shards(): jnp.take(gathered[1], mine_index, axis=1) * mine_mask[None, :, None]  11.9 us
    dot_general x1, matrix products, shards(): jnp.einsum('mcy,cxy->mcx', weight_cols, covariance, preferred_element_typ...  11.7 us
    convert_element_type x1, other arithmetic, shards(): pred_pert = (pred_rows - mean_pred).astype(jnp.bfloat16).reshape(total_me...  11 us
    gather x2, local copies, waits for them, and re-layouts, shards(): jnp.take(background_trajectories, tile_at_place, axis=1)  8.62 us
    reduce_sum x1, other arithmetic, shards(): mean_pred = jnp.mean(pred_rows, axis=0, dtype=jnp.float32)  7.51 us
  transfers between devices with their start and end apart: 4, of which 3 were waited for; matrix products, arithmetic and copies ran while one was open for 25% of the time, Pallas kernels for 0%

commit v1 on v0

--- a/solution.py
+++ b/solution.py
@@ -1,10 +1,229 @@
+import functools
+
 import jax
 import jax.numpy as jnp
 from jax import lax
+from jax.experimental import pallas as pl
+from jax.experimental.pallas import tpu as pltpu
 from jax.sharding import PartitionSpec as P
 
 REACH = 12
 CAP = 2
+MESH = pl.DeviceIdType.MESH
+EXACT = lax.Precision.HIGHEST
+
+
+def exchange(
+    mem, lev,
+    tile_ref, live_ref, bg_ref, map_ref, sensed_ref, precision_ref,
+    pw_ref, st_ref,
+    half, outgoing, part, arrived,
+    part_send, part_recv, state_send, state_recv, mem_send, mem_recv,
+    y_send, y_recv, core_send, core_recv,
+):
+    me, lv = lax.axis_index("mem"), lax.axis_index("lev")
+    blocks, members = half.shape[0], half.shape[1]
+    layers = map_ref.shape[0]
+    rows = members // lev
+    mem_peers = [lax.rem(me + d, mem) for d in range(1, mem)]
+    lev_peers = [lax.rem(lv + d, lev) for d in range(1, lev)]
+    core = lv + 1 - 2 * lax.rem(lv, 2)
+    across = lax.rem(lv + 2, lev)
+
+    barrier = pltpu.get_barrier_semaphore()
+    for k in mem_peers:
+        pl.semaphore_signal(barrier, inc=1, device_id=(k, lv), device_id_type=MESH)
+    for k in lev_peers:
+        pl.semaphore_signal(barrier, inc=1, device_id=(me, k), device_id_type=MESH)
+
+    for b in range(blocks):
+        total = None
+        for h in range(layers):
+            piece = bg_ref[pl.ds(b * layers + h, members, stride=blocks * layers), :]
+            half[b, :, h * 128:(h + 1) * 128] = piece.astype(jnp.bfloat16)
+            term = jnp.dot(piece, map_ref[h], precision=EXACT, preferred_element_type=jnp.float32)
+            total = term if total is None else total + term
+        for q in range(lev):
+            part[q, b] = total[q * rows:(q + 1) * rows]
+
+    pl.semaphore_wait(barrier, mem - 1 + lev - 1)
+
+    copies = []
+    part_copies = []
+    for d in range(1, lev):
+        to = lev_peers[d - 1]
+        c = pltpu.make_async_remote_copy(
+            part.at[to], arrived.at[d], part_send.at[d], part_recv.at[d],
+            device_id=(me, to), device_id_type=MESH)
+        c.start()
+        part_copies.append(c)
+
+    state_copies = []
+    for d in range(1, mem):
+        to = mem_peers[d - 1]
+        for c in range(CAP):
+            slot = to * CAP + c
+            outgoing[d, c] = half[tile_ref[slot]] * live_ref[slot].astype(jnp.bfloat16)
+        c = pltpu.make_async_remote_copy(
+            outgoing.at[d], st_ref.at[me], state_send.at[d], state_recv.at[d],
+            device_id=(to, lv), device_id_type=MESH)
+        c.start()
+        state_copies.append(c)
+    for c in range(CAP):
+        slot = me * CAP + c
+        st_ref[me, c] = half[tile_ref[slot]] * live_ref[slot].astype(jnp.bfloat16)
+
+    for c in part_copies:
+        c.wait_recv()
+    for b in range(blocks):
+        pred = part[lv, b]
+        for d in range(1, lev):
+            pred = pred + arrived[d, b]
+        pw_ref[me, lv, 0, b] = pred.astype(jnp.bfloat16)
+        gap = sensed_ref[pl.ds(lv * rows * blocks + b, rows, stride=blocks), :] - pred
+        pw_ref[me, lv, 1, b] = jnp.dot(
+            gap, precision_ref[b], precision=EXACT, preferred_element_type=jnp.float32
+        ).astype(jnp.bfloat16)
+
+    def pass_on(owner, quarter, send, recv, to):
+        return pltpu.make_async_remote_copy(
+            pw_ref.at[owner, quarter], pw_ref.at[owner, quarter], send, recv,
+            device_id=to, device_id_type=MESH)
+
+    mem_copies = []
+    for d in range(1, mem):
+        c = pass_on(me, lv, mem_send.at[d], mem_recv.at[d], (mem_peers[d - 1], lv))
+        c.start()
+        mem_copies.append(c)
+    y_copies, core_copies = [], []
+    for d in range(mem):
+        source = lax.rem(me + mem - d, mem)
+        if d > 0:
+            pltpu.make_async_remote_copy(
+                pw_ref.at[source, lv], pw_ref.at[source, lv], mem_send.at[d], mem_recv.at[d],
+                device_id=(source, lv), device_id_type=MESH).wait_recv()
+        c = pass_on(source, lv, y_send.at[d], y_recv.at[d], (me, across))
+        c.start()
+        y_copies.append(c)
+        c = pass_on(source, lv, core_send.at[0, d], core_recv.at[0, d], (me, core))
+        c.start()
+        core_copies.append(c)
+    for d in range(mem):
+        source = lax.rem(me + mem - d, mem)
+        pass_on(source, across, y_send.at[d], y_recv.at[d], (me, across)).wait_recv()
+        c = pass_on(source, across, core_send.at[1, d], core_recv.at[1, d], (me, core))
+        c.start()
+        core_copies.append(c)
+    other = lax.rem(core + 2, lev)
+    for d in range(mem):
+        source = lax.rem(me + mem - d, mem)
+        pass_on(source, core, core_send.at[0, d], core_recv.at[0, d], (me, core)).wait_recv()
+        pass_on(source, other, core_send.at[1, d], core_recv.at[1, d], (me, core)).wait_recv()
+    for d in range(1, mem):
+        source = lax.rem(me + mem - d, mem)
+        pltpu.make_async_remote_copy(
+            outgoing.at[d], st_ref.at[source], state_send.at[d], state_recv.at[d],
+            device_id=(source, lv), device_id_type=MESH).wait_recv()
+    for c in part_copies + state_copies + mem_copies + y_copies + core_copies:
+        c.wait_send()
+
+
+def analyse(scale_ref, pw_ref, st_ref, out_ref, covariance):
+    mem, lev, _, blocks, rows, obs = pw_ref.shape
+    capacity, members, width = st_ref.shape[1:]
+    total = mem * members
+
+    @pl.loop(0, blocks)
+    def _(b):
+        pred = pw_ref[:, :, 0, b].reshape(total, obs).astype(jnp.float32)
+        mean = jnp.sum(pred, axis=0, keepdims=True) * (1.0 / total)
+        pert = (pred - mean).astype(jnp.bfloat16)
+        for c in range(capacity):
+            cov = lax.dot_general(
+                pert, st_ref[:, c].reshape(total, width), (((0,), (0,)), ((), ())),
+                preferred_element_type=jnp.float32)
+            covariance[pl.ds(pl.multiple_of(b * obs, obs), obs), c * width:(c + 1) * width] = (
+                cov * scale_ref[c * blocks + b]).astype(jnp.bfloat16)
+
+    parts = 4 if mem % 4 == 0 else mem
+    chunk = mem // parts
+
+    @pl.loop(0, parts)
+    def _(r):
+        owners = pl.ds(r * chunk, chunk)
+        weighted = jnp.concatenate(
+            [pw_ref[owners, :, 1, b].reshape(chunk * members, obs) for b in range(blocks)], axis=1)
+        per_slot = width // 128
+        for c in range(capacity):
+            rise = jnp.dot(
+                weighted, covariance[:, c * width:(c + 1) * width],
+                preferred_element_type=jnp.float32)
+            value = st_ref[owners, c].reshape(chunk * members, width).astype(jnp.float32) + rise
+            for h in range(per_slot):
+                stride = capacity * per_slot
+                start = r * chunk * members * stride + c * per_slot + h
+                out_ref[pl.ds(start, chunk * members, stride=stride), :] = (
+                    value[:, h * 128:(h + 1) * 128])
+
+
+def dense_shards(mem, lev, bg, linear_map, sensed, precision, table, holder_rank):
+    members, blocks, layers, sites = bg.shape
+    obs = linear_map.shape[2]
+    rows = members // lev
+    width = layers * sites
+    me = lax.axis_index("mem")
+    block_ids = jnp.arange(blocks, dtype=jnp.int32)
+    same = holder_rank[:, None] == holder_rank[None, :]
+    earlier = block_ids[None, :] < block_ids[:, None]
+    slot_of = holder_rank * CAP + jnp.sum((same & earlier).astype(jnp.int32), axis=1)
+    slot_ids = jnp.arange(mem * CAP, dtype=jnp.int32)
+    matches = slot_of[None, :] == slot_ids[:, None]
+    live = jnp.any(matches, axis=1).astype(jnp.float32)
+    tile = jnp.sum(jnp.where(matches, block_ids[None, :], 0), axis=1)
+    away = jnp.abs(block_ids[:, None] - block_ids[None, :])
+    gap = 2.0 * jnp.minimum(away, blocks - away).astype(jnp.float32) / REACH
+    times = jnp.sum((table[:, :, None] == block_ids[None, None, :]).astype(jnp.float32), axis=1)
+    weights = times / (1.0 + gap * gap) / (mem * members - 1)
+    mine = (slot_of[None, :] == (me * CAP + jnp.arange(CAP, dtype=jnp.int32))[:, None])
+    scale = jnp.sum(jnp.where(mine[:, :, None], weights[None], 0.0), axis=1).reshape(-1)
+
+    smem = pl.BlockSpec(memory_space=pltpu.SMEM)
+    vmem = pl.BlockSpec(memory_space=pltpu.VMEM)
+    dma = pltpu.SemaphoreType.DMA
+    half = jnp.bfloat16
+    pw, st = pl.pallas_call(
+        functools.partial(exchange, mem, lev),
+        out_shape=(
+            jax.ShapeDtypeStruct((mem, lev, 2, blocks, rows, obs), half),
+            jax.ShapeDtypeStruct((mem, CAP, members, width), half),
+        ),
+        in_specs=[smem, smem, vmem, vmem, vmem, vmem],
+        out_specs=(vmem, vmem),
+        scratch_shapes=[
+            pltpu.VMEM((blocks, members, width), half),
+            pltpu.VMEM((mem, CAP, members, width), half),
+            pltpu.VMEM((lev, blocks, rows, obs), jnp.float32),
+            pltpu.VMEM((lev, blocks, rows, obs), jnp.float32),
+            dma((lev,)), dma((lev,)), dma((mem,)), dma((mem,)), dma((mem,)), dma((mem,)),
+            dma((mem,)), dma((mem,)), dma((2, mem)), dma((2, mem)),
+        ],
+        compiler_params=pltpu.CompilerParams(
+            collective_id=0, has_side_effects=True, vmem_limit_bytes=40 * 2**20),
+        name="exchange",
+    )(
+        tile, live, bg.reshape(members * blocks * layers, sites), linear_map,
+        sensed.reshape(members * blocks, obs), precision,
+    )
+    out = pl.pallas_call(
+        analyse,
+        out_shape=jax.ShapeDtypeStruct((mem * members * CAP * layers, sites), jnp.float32),
+        in_specs=[smem, vmem, vmem],
+        out_specs=vmem,
+        scratch_shapes=[pltpu.VMEM((blocks * obs, CAP * width), half)],
+        compiler_params=pltpu.CompilerParams(vmem_limit_bytes=40 * 2**20),
+        name="analyse",
+    )(scale, pw, st)
+    return out.reshape(mem * members, CAP, layers, sites)
 
 
 def shards(
@@ -99,4 +318,11 @@
         P(),
     )
     out_specs = P(None, "mem", "lev", None)
-    return jax.shard_map(shards, mesh=mesh, in_specs=in_specs, out_specs=out_specs, check_vma=False)
+    mem, lev = mesh.shape["mem"], mesh.shape["lev"]
+
+    def local(bg, linear_map, sensed, precision, table, holder_rank):
+        dense = bg.shape[1] <= table.shape[1] and lev == 4 and bg.shape[0] % 64 == 0
+        body = functools.partial(dense_shards, mem, lev) if dense else shards
+        return body(bg, linear_map, sensed, precision, table, holder_rank)
+
+    return jax.shard_map(local, mesh=mesh, in_specs=in_specs, out_specs=out_specs, check_vma=False)

time: 228 us -> 79.7 us (0.35)
  the two profiles are of different devices: /device:TPU:0 before, /device:TPU:17 now
where the time goes in v1:
time: 79.7 us; the launch traced here: 79.4 us
  Pallas kernels  72.4 us (91%)
  local copies, waits for them, and re-layouts  4.3 us (5%)
  other arithmetic  2.7 us (3%)
    pallas_call x1, Pallas kernels, dense_shards(): pl.pallas_call(functools.partial(exchange, mem, lev), out_shape=(jax.Shap...  64.9 us
    pallas_call x1, Pallas kernels, dense_shards(): pl.pallas_call(analyse, out_shape=jax.ShapeDtypeStruct((mem * members * C...  7.44 us
    unnamed x8, local copies, waits for them, and re-layouts  4.22 us

profile of v1, /device:TPU:17, one launch (start us, length us, event | category | flops | bytes accessed | tf_op | source)
XLA Modules:
  0.0 79.4 jit_solution(492034507463391555)
XLA Ops:
  0.0 0.9 %convert_reduce_fusion.1 = s32[8]{0:T(128)S(1)} fusion(s32[8]{0:T(128)} %param.11), kind=kLoop, calls=%fused_computation.13 | loop fusion | flops 312 | bytes 64 | tf_op jit(solution)/shard_map/reduce_sum | solution.py:178
  0.9 0.7 multiply_add_fusion
  1.6 0.1 broadcast_compare_fusion
  1.7 0.1 fusion.6
  1.7 0.1 select_reduce_fusion.1.tile_ref
  1.8 0.8 convert_reduce_fusion
  2.6 0.1 select_reduce_fusion
  2.7 0.1 reshape.68.scale_ref
  2.8 0.0 copy-start
  2.8 1.2 %copy-done = f32[128,8,2,128]{3,2,1,0:T(2,128)S(1)} copy-done((f32[128,8,2,128]{3,2,1,0:T(2,128)S(1)}, f32[128,8,2,128]{3,2,1,0:T(2,128)}, u32[]{:S(2)}) %copy-start) | copy-done | bytes 1048600
  4.0 0.0 copy-start.1
  4.0 1.0 %copy-done.1 = f32[128,8,128]{2,1,0:T(8,128)S(1)} copy-done((f32[128,8,128]{2,1,0:T(8,128)S(1)}, f32[128,8,128]{2,1,0:T(8,128)}, u32[]{:S(2)}) %copy-start.1) | copy-done | bytes 524312
  5.1 0.0 copy-start.2
  5.1 1.0 %copy-done.2 = f32[8,128,128]{2,1,0:T(8,128)S(1)} copy-done((f32[8,128,128]{2,1,0:T(8,128)S(1)}, f32[8,128,128]{2,1,0:T(8,128)}, u32[]{:S(2)}) %copy-start.2) | copy-done | bytes 524312
  6.1 0.0 copy-start.3
  6.1 0.9 %copy-done.3 = f32[2,128,128]{2,1,0:T(8,128)S(1)} copy-done((f32[2,128,128]{2,1,0:T(8,128)S(1)}, f32[2,128,128]{2,1,0:T(8,128)}, u32[]{:S(2)}) %copy-start.3) | copy-done | bytes 131096
  7.0 64.9 %exchange.1 = (bf16[8,4,2,8,32,128]{5,4,3,2,1,0:T(8,128)(2,1)S(1)}, bf16[8,2,128,256]{3,2,1,0:T(8,128)(2,1)S(1)}) custom-call(s32[16]{0:T(128)S(1)} %select_reduce_fusion.1.tile_ref, f32[16]{0:T(128)S(1)} %convert_element_type.19.live_ref, f32[2048,128]{1,0:T(8,128)S(1)} %bitcast.3, f32[2,128,128]{2,1,0:T(8,128)S(1)} %copy-done.3, f32[1024,128]{1,0:T(8,128)S(1)} %bitcast.4, ...), custom_call_target="tpu_custom_call" | custom-call | tf_op jit(solution)/shard_map/exchange/pallas_call | solution.py:194
  72.0 7.4 %analyse.1 = f32[4096,128]{1,0:T(8,128)} custom-call(f32[16]{0:T(128)S(1)} %reshape.68.scale_ref, bf16[8,4,2,8,32,128]{5,4,3,2,1,0:T(8,128)(2,1)S(1)} %get-tuple-element.7.pw_ref, bf16[8,2,128,256]{3,2,1,0:T(8,128)(2,1)S(1)} %get-tuple-element.8.st_ref), custom_call_target="tpu_custom_call" | custom-call | tf_op jit(solution)/shard_map/analyse/pallas_call | solution.py:217
  (3 shorter events, 0.0 us)
Async XLA Ops:
  2.8 1.2 %copy-start = (f32[128,8,2,128]{3,2,1,0:T(2,128)S(1)}, f32[128,8,2,128]{3,2,1,0:T(2,128)}, u32[]{:S(2)}) copy-start(f32[128,8,2,128]{3,2,1,0:T(2,128)} %param.6) | copy-start | bytes 3145732
  4.0 1.0 %copy-start.1 = (f32[128,8,128]{2,1,0:T(8,128)S(1)}, f32[128,8,128]{2,1,0:T(8,128)}, u32[]{:S(2)}) copy-start(f32[128,8,128]{2,1,0:T(8,128)} %param.8) | copy-start | bytes 1572868
  5.1 1.0 %copy-start.2 = (f32[8,128,128]{2,1,0:T(8,128)S(1)}, f32[8,128,128]{2,1,0:T(8,128)}, u32[]{:S(2)}) copy-start(f32[8,128,128]{2,1,0:T(8,128)} %precision_ref.1) | copy-start | bytes 1572868
  6.1 0.9 %copy-start.3 = (f32[2,128,128]{2,1,0:T(8,128)S(1)}, f32[2,128,128]{2,1,0:T(8,128)}, u32[]{:S(2)}) copy-start(f32[2,128,128]{2,1,0:T(8,128)} %map_ref.1) | copy-start | bytes 393220

commit v2 on v1

--- a/solution.py
+++ b/solution.py
@@ -13,12 +13,25 @@
 EXACT = lax.Precision.HIGHEST
 
 
+def split(value):
+    high = value.astype(jnp.bfloat16)
+    return high, (value - high.astype(jnp.float32)).astype(jnp.bfloat16)
+
+
+def split_dot(left, right_pair):
+    rows, cols = left.shape[0], right_pair.shape[1] // 2
+    both = jnp.dot(
+        jnp.concatenate(split(left), axis=0), right_pair, preferred_element_type=jnp.float32)
+    return both[:rows, :cols] + (both[:rows, cols:] + both[rows:, :cols])
+
+
 def exchange(
     mem, lev,
-    tile_ref, live_ref, bg_ref, map_ref, sensed_ref, precision_ref,
-    pw_ref, st_ref,
-    half, outgoing, part, arrived,
-    part_send, part_recv, state_send, state_recv, mem_send, mem_recv,
+    holder_ref, table_ref, bg_hbm, map_hbm, sensed_hbm, precision_hbm,
+    pw_ref, st_ref, scale_ref,
+    bg_ref, map_ref, sensed_ref, precision_ref, local_sem,
+    half, outgoing, part, arrived, pairs,
+    part_send, part_recv, state_send, state_recv, z_send, z_recv, x_send, x_recv,
     y_send, y_recv, core_send, core_recv,
 ):
     me, lv = lax.axis_index("mem"), lax.axis_index("lev")
@@ -29,6 +42,10 @@
     lev_peers = [lax.rem(lv + d, lev) for d in range(1, lev)]
     core = lv + 1 - 2 * lax.rem(lv, 2)
     across = lax.rem(lv + 2, lev)
+    other = lax.rem(core + 2, lev)
+    depth = mem // 2
+    x = lax.rem(me, 2)
+    side = me + 1 - 2 * x
 
     barrier = pltpu.get_barrier_semaphore()
     for k in mem_peers:
@@ -36,13 +53,38 @@
     for k in lev_peers:
         pl.semaphore_signal(barrier, inc=1, device_id=(me, k), device_id_type=MESH)
 
+    loads = []
+    for i, (src, dst) in enumerate((
+            (map_hbm, map_ref), (bg_hbm, bg_ref),
+            (sensed_hbm, sensed_ref), (precision_hbm, precision_ref))):
+        c = pltpu.make_async_copy(src, dst, local_sem.at[i])
+        c.start()
+        loads.append(c)
+
+    holder = [holder_ref[b] for b in range(blocks)]
+    order = [
+        sum(((holder[e] == holder[b]).astype(jnp.int32) for e in range(b)), jnp.int32(0))
+        for b in range(blocks)]
+    slot_of = [holder[b] * CAP + order[b] for b in range(blocks)]
+
+    def find(slot):
+        tile, live = jnp.int32(0), jnp.int32(0)
+        for b in range(blocks):
+            hit = slot_of[b] == slot
+            tile = jnp.where(hit, b, tile)
+            live = jnp.where(hit, 1, live)
+        return tile, live.astype(jnp.float32)
+
+    loads[0].wait()
+    loads[1].wait()
+    table_pair = jnp.concatenate(
+        [jnp.concatenate(split(map_ref[h]), axis=1) for h in range(layers)], axis=0)
     for b in range(blocks):
-        total = None
-        for h in range(layers):
-            piece = bg_ref[pl.ds(b * layers + h, members, stride=blocks * layers), :]
-            half[b, :, h * 128:(h + 1) * 128] = piece.astype(jnp.bfloat16)
-            term = jnp.dot(piece, map_ref[h], precision=EXACT, preferred_element_type=jnp.float32)
-            total = term if total is None else total + term
+        state = jnp.concatenate([
+            bg_ref[pl.ds(b * layers + h, members, stride=blocks * layers), :]
+            for h in range(layers)], axis=1)
+        half[b] = state.astype(jnp.bfloat16)
+        total = split_dot(state, table_pair)
         for q in range(lev):
             part[q, b] = total[q * rows:(q + 1) * rows]
 
@@ -58,21 +100,28 @@
         c.start()
         part_copies.append(c)
 
-    state_copies = []
-    for d in range(1, mem):
-        to = mem_peers[d - 1]
-        for c in range(CAP):
-            slot = to * CAP + c
-            outgoing[d, c] = half[tile_ref[slot]] * live_ref[slot].astype(jnp.bfloat16)
-        c = pltpu.make_async_remote_copy(
-            outgoing.at[d], st_ref.at[me], state_send.at[d], state_recv.at[d],
-            device_id=(to, lv), device_id_type=MESH)
-        c.start()
-        state_copies.append(c)
+    def send_states(distances):
+        for d in distances:
+            to = mem_peers[d - 1]
+            for c in range(CAP):
+                tile, live = find(to * CAP + c)
+                outgoing[d, c] = half[tile] * live.astype(jnp.bfloat16)
+            copy = pltpu.make_async_remote_copy(
+                outgoing.at[d], st_ref.at[me], state_send.at[d], state_recv.at[d],
+                device_id=(to, lv), device_id_type=MESH)
+            copy.start()
+            copies.append(copy)
+
+    early = [d for d in range(1, mem) if d in (depth, depth + 1)]
+    send_states(early)
     for c in range(CAP):
-        slot = me * CAP + c
-        st_ref[me, c] = half[tile_ref[slot]] * live_ref[slot].astype(jnp.bfloat16)
-
+        tile, live = find(me * CAP + c)
+        st_ref[me, c] = half[tile] * live.astype(jnp.bfloat16)
+
+    loads[2].wait()
+    loads[3].wait()
+    for b in range(blocks):
+        pairs[b] = jnp.concatenate(split(precision_ref[b]), axis=1)
     for c in part_copies:
         c.wait_recv()
     for b in range(blocks):
@@ -81,50 +130,67 @@
             pred = pred + arrived[d, b]
         pw_ref[me, lv, 0, b] = pred.astype(jnp.bfloat16)
         gap = sensed_ref[pl.ds(lv * rows * blocks + b, rows, stride=blocks), :] - pred
-        pw_ref[me, lv, 1, b] = jnp.dot(
-            gap, precision_ref[b], precision=EXACT, preferred_element_type=jnp.float32
-        ).astype(jnp.bfloat16)
+        pw_ref[me, lv, 1, b] = split_dot(gap, pairs[b]).astype(jnp.bfloat16)
 
     def pass_on(owner, quarter, send, recv, to):
         return pltpu.make_async_remote_copy(
             pw_ref.at[owner, quarter], pw_ref.at[owner, quarter], send, recv,
             device_id=to, device_id_type=MESH)
 
-    mem_copies = []
-    for d in range(1, mem):
-        c = pass_on(me, lv, mem_send.at[d], mem_recv.at[d], (mem_peers[d - 1], lv))
+    def begin(*args):
+        c = pass_on(*args)
         c.start()
-        mem_copies.append(c)
-    y_copies, core_copies = [], []
-    for d in range(mem):
-        source = lax.rem(me + mem - d, mem)
-        if d > 0:
-            pltpu.make_async_remote_copy(
-                pw_ref.at[source, lv], pw_ref.at[source, lv], mem_send.at[d], mem_recv.at[d],
-                device_id=(source, lv), device_id_type=MESH).wait_recv()
-        c = pass_on(source, lv, y_send.at[d], y_recv.at[d], (me, across))
-        c.start()
-        y_copies.append(c)
-        c = pass_on(source, lv, core_send.at[0, d], core_recv.at[0, d], (me, core))
-        c.start()
-        core_copies.append(c)
-    for d in range(mem):
-        source = lax.rem(me + mem - d, mem)
-        pass_on(source, across, y_send.at[d], y_recv.at[d], (me, across)).wait_recv()
-        c = pass_on(source, across, core_send.at[1, d], core_recv.at[1, d], (me, core))
-        c.start()
-        core_copies.append(c)
-    other = lax.rem(core + 2, lev)
-    for d in range(mem):
-        source = lax.rem(me + mem - d, mem)
-        pass_on(source, core, core_send.at[0, d], core_recv.at[0, d], (me, core)).wait_recv()
-        pass_on(source, other, core_send.at[1, d], core_recv.at[1, d], (me, core)).wait_recv()
+        copies.append(c)
+
+    near = [lax.rem(me + mem - 2 * d, mem) for d in range(depth)]
+    far = [lax.rem(side + mem - 2 * d, mem) for d in range(depth)]
+    owners = near + far
+    for d in range(1, depth):
+        begin(me, lv, z_send.at[d], z_recv.at[d], (lax.rem(me + 2 * d, mem), lv))
+
+    def spread(e):
+        begin(owners[e], lv, y_send.at[e], y_recv.at[e], (me, across))
+        begin(owners[e], lv, core_send.at[0, e], core_recv.at[0, e], (me, core))
+
+    begin(me, lv, x_send.at[0], x_recv.at[0], (side, lv))
+    spread(0)
+    send_states([d for d in range(1, mem) if d not in early])
+    pass_on(far[0], lv, x_send.at[0], x_recv.at[0], (side, lv)).wait_recv()
+    spread(depth)
+    for d in range(1, depth):
+        pass_on(near[d], lv, z_send.at[d], z_recv.at[d], (near[d], lv)).wait_recv()
+        begin(near[d], lv, x_send.at[d], x_recv.at[d], (side, lv))
+        spread(d)
+        pass_on(far[d], lv, x_send.at[d], x_recv.at[d], (side, lv)).wait_recv()
+        spread(depth + d)
+
+    here = [find(me * CAP + c) for c in range(CAP)]
+    for c in range(CAP):
+        tile, live = here[c]
+        listed = [table_ref[tile, q] for q in range(table_ref.shape[1])]
+        for b in range(blocks):
+            times = sum(((entry == b).astype(jnp.int32) for entry in listed), jnp.int32(0))
+            away = jnp.abs(tile - b)
+            gap = jnp.minimum(away, blocks - away)
+            weight = jnp.float32(0)
+            for g in range(blocks // 2 + 1):
+                value = 1.0 / (1.0 + (2.0 * g / REACH) ** 2) / (mem * members - 1)
+                weight = jnp.where(gap == g, jnp.float32(value), weight)
+            scale_ref[c * blocks + b] = times.astype(jnp.float32) * weight * live
+
+    turns = [0, depth] + [e for d in range(1, depth) for e in (d, depth + d)]
+    for e in turns:
+        pass_on(owners[e], across, y_send.at[e], y_recv.at[e], (me, across)).wait_recv()
+        begin(owners[e], across, core_send.at[1, e], core_recv.at[1, e], (me, core))
+    for e in turns:
+        pass_on(owners[e], core, core_send.at[0, e], core_recv.at[0, e], (me, core)).wait_recv()
+        pass_on(owners[e], other, core_send.at[1, e], core_recv.at[1, e], (me, core)).wait_recv()
     for d in range(1, mem):
         source = lax.rem(me + mem - d, mem)
         pltpu.make_async_remote_copy(
             outgoing.at[d], st_ref.at[source], state_send.at[d], state_recv.at[d],
             device_id=(source, lv), device_id_type=MESH).wait_recv()
-    for c in part_copies + state_copies + mem_copies + y_copies + core_copies:
+    for c in part_copies + copies:
         c.wait_send()
 
 
@@ -171,47 +237,41 @@
     obs = linear_map.shape[2]
     rows = members // lev
     width = layers * sites
-    me = lax.axis_index("mem")
-    block_ids = jnp.arange(blocks, dtype=jnp.int32)
-    same = holder_rank[:, None] == holder_rank[None, :]
-    earlier = block_ids[None, :] < block_ids[:, None]
-    slot_of = holder_rank * CAP + jnp.sum((same & earlier).astype(jnp.int32), axis=1)
-    slot_ids = jnp.arange(mem * CAP, dtype=jnp.int32)
-    matches = slot_of[None, :] == slot_ids[:, None]
-    live = jnp.any(matches, axis=1).astype(jnp.float32)
-    tile = jnp.sum(jnp.where(matches, block_ids[None, :], 0), axis=1)
-    away = jnp.abs(block_ids[:, None] - block_ids[None, :])
-    gap = 2.0 * jnp.minimum(away, blocks - away).astype(jnp.float32) / REACH
-    times = jnp.sum((table[:, :, None] == block_ids[None, None, :]).astype(jnp.float32), axis=1)
-    weights = times / (1.0 + gap * gap) / (mem * members - 1)
-    mine = (slot_of[None, :] == (me * CAP + jnp.arange(CAP, dtype=jnp.int32))[:, None])
-    scale = jnp.sum(jnp.where(mine[:, :, None], weights[None], 0.0), axis=1).reshape(-1)
-
     smem = pl.BlockSpec(memory_space=pltpu.SMEM)
     vmem = pl.BlockSpec(memory_space=pltpu.VMEM)
+    hbm = pl.BlockSpec(memory_space=pltpu.HBM)
     dma = pltpu.SemaphoreType.DMA
     half = jnp.bfloat16
-    pw, st = pl.pallas_call(
+    wide = jnp.float32
+    pw, st, scale = pl.pallas_call(
         functools.partial(exchange, mem, lev),
         out_shape=(
             jax.ShapeDtypeStruct((mem, lev, 2, blocks, rows, obs), half),
             jax.ShapeDtypeStruct((mem, CAP, members, width), half),
+            jax.ShapeDtypeStruct((CAP * blocks,), wide),
         ),
-        in_specs=[smem, smem, vmem, vmem, vmem, vmem],
-        out_specs=(vmem, vmem),
+        in_specs=[smem, smem, hbm, hbm, hbm, hbm],
+        out_specs=(vmem, vmem, smem),
         scratch_shapes=[
+            pltpu.VMEM((members * blocks * layers, sites), wide),
+            pltpu.VMEM(linear_map.shape, wide),
+            pltpu.VMEM((members * blocks, obs), wide),
+            pltpu.VMEM(precision.shape, wide),
+            dma((4,)),
             pltpu.VMEM((blocks, members, width), half),
             pltpu.VMEM((mem, CAP, members, width), half),
-            pltpu.VMEM((lev, blocks, rows, obs), jnp.float32),
-            pltpu.VMEM((lev, blocks, rows, obs), jnp.float32),
-            dma((lev,)), dma((lev,)), dma((mem,)), dma((mem,)), dma((mem,)), dma((mem,)),
+            pltpu.VMEM((lev, blocks, rows, obs), wide),
+            pltpu.VMEM((lev, blocks, rows, obs), wide),
+            pltpu.VMEM((blocks, obs, 2 * obs), half),
+            dma((lev,)), dma((lev,)), dma((mem,)), dma((mem,)),
+            dma((mem,)), dma((mem,)), dma((mem,)), dma((mem,)),
             dma((mem,)), dma((mem,)), dma((2, mem)), dma((2, mem)),
         ],
         compiler_params=pltpu.CompilerParams(
             collective_id=0, has_side_effects=True, vmem_limit_bytes=40 * 2**20),
         name="exchange",
     )(
-        tile, live, bg.reshape(members * blocks * layers, sites), linear_map,
+        holder_rank, table, bg.reshape(members * blocks * layers, sites), linear_map,
         sensed.reshape(members * blocks, obs), precision,
     )
     out = pl.pallas_call(
@@ -321,7 +381,7 @@
     mem, lev = mesh.shape["mem"], mesh.shape["lev"]
 
     def local(bg, linear_map, sensed, precision, table, holder_rank):
-        dense = bg.shape[1] <= table.shape[1] and lev == 4 and bg.shape[0] % 64 == 0
+        dense = bg.shape[1] <= table.shape[1] and lev == 4 and mem % 2 == 0 and bg.shape[0] % 64 == 0
         body = functools.partial(dense_shards, mem, lev) if dense else shards
         return body(bg, linear_map, sensed, precision, table, holder_rank)
 

time: 79.7 us -> 65.4 us (0.82)
  the two profiles are of different devices: /device:TPU:17 before, /device:TPU:0 now
where the time goes in v2:
time: 65.4 us; the launch traced here: 65.1 us
  Pallas kernels  59.5 us (91%)
  local copies, waits for them, and re-layouts  5.55 us (8%)
    pallas_call x1, Pallas kernels, dense_shards(): pl.pallas_call(functools.partial(exchange, mem, lev), out_shape=(jax.Shap...  52.1 us
    pallas_call x1, Pallas kernels, dense_shards(): pl.pallas_call(analyse, out_shape=jax.ShapeDtypeStruct((mem * members * C...  7.44 us
    unnamed x12, local copies, waits for them, and re-layouts  5.55 us

profile of v2, /device:TPU:0, one launch (start us, length us, event | category | flops | bytes accessed | tf_op | source)
XLA Modules:
  0.0 65.1 jit_solution(8682834720173278304)
XLA Ops:
  0.0 0.0 copy-start
  0.0 1.2 %copy-done = f32[128,8,2,128]{3,2,1,0:T(2,128)S(1)} copy-done((f32[128,8,2,128]{3,2,1,0:T(2,128)S(1)}, f32[128,8,2,128]{3,2,1,0:T(2,128)}, u32[]{:S(2)}) %copy-start) | copy-done | bytes 1048600
  1.2 0.0 copy-start.1
  1.2 1.0 %copy-done.1 = f32[128,8,128]{2,1,0:T(8,128)S(1)} copy-done((f32[128,8,128]{2,1,0:T(8,128)S(1)}, f32[128,8,128]{2,1,0:T(8,128)}, u32[]{:S(2)}) %copy-start.1) | copy-done | bytes 524312
  2.3 0.0 copy-start.2
  2.3 1.0 %copy-done.2 = f32[8,128,128]{2,1,0:T(8,128)S(1)} copy-done((f32[8,128,128]{2,1,0:T(8,128)S(1)}, f32[8,128,128]{2,1,0:T(8,128)}, u32[]{:S(2)}) %copy-start.2) | copy-done | bytes 524312
  3.3 0.0 copy-start.3
  3.3 0.9 %copy-done.3 = f32[2,128,128]{2,1,0:T(8,128)S(1)} copy-done((f32[2,128,128]{2,1,0:T(8,128)S(1)}, f32[2,128,128]{2,1,0:T(8,128)}, u32[]{:S(2)}) %copy-start.3) | copy-done | bytes 131096
  4.2 0.0 copy-start.4
  4.2 0.7 %copy-done.4 = s32[8,16]{1,0:T(8,128)S(1)} copy-done((s32[8,16]{1,0:T(8,128)S(1)}, s32[8,16]{1,0:T(8,128)}, u32[]{:S(2)}) %copy-start.4) | copy-done | bytes 536
  4.9 0.0 copy-start.5
  4.9 0.7 %copy-done.5 = s32[8]{0:T(128)S(1)} copy-done((s32[8]{0:T(128)S(1)}, s32[8]{0:T(128)}, u32[]{:S(2)}) %copy-start.5) | copy-done | bytes 56
  5.6 52.1 %exchange.1 = (bf16[8,4,2,8,32,128]{5,4,3,2,1,0:T(8,128)(2,1)S(1)}, bf16[8,2,128,256]{3,2,1,0:T(8,128)(2,1)S(1)}, f32[16]{0:T(128)S(1)}) custom-call(s32[8]{0:T(128)S(1)} %copy-done.5, s32[8,16]{1,0:T(8,128)S(1)} %copy-done.4, f32[2048,128]{1,0:T(8,128)S(1)} %bitcast.3, f32[2,128,128]{2,1,0:T(8,128)S(1)} %copy-done.3, f32[1024,128]{1,0:T(8,128)S(1)} %bitcast.4, ...), custom_call_target="tpu_custom_call" | custom-call | tf_op jit(solution)/shard_map/exchange/pallas_call | solution.py:246
  57.7 7.4 %analyse.1 = f32[4096,128]{1,0:T(8,128)} custom-call(f32[16]{0:T(128)S(1)} %get-tuple-element.8.scale_ref, bf16[8,4,2,8,32,128]{5,4,3,2,1,0:T(8,128)(2,1)S(1)} %get-tuple-element.9.pw_ref, bf16[8,2,128,256]{3,2,1,0:T(8,128)(2,1)S(1)} %get-tuple-element.10.st_ref), custom_call_target="tpu_custom_call" | custom-call | tf_op jit(solution)/shard_map/analyse/pallas_call | solution.py:277
Async XLA Ops:
  0.0 1.2 %copy-start = (f32[128,8,2,128]{3,2,1,0:T(2,128)S(1)}, f32[128,8,2,128]{3,2,1,0:T(2,128)}, u32[]{:S(2)}) copy-start(f32[128,8,2,128]{3,2,1,0:T(2,128)} %param.6) | copy-start | bytes 3145732
  1.2 1.0 %copy-start.1 = (f32[128,8,128]{2,1,0:T(8,128)S(1)}, f32[128,8,128]{2,1,0:T(8,128)}, u32[]{:S(2)}) copy-start(f32[128,8,128]{2,1,0:T(8,128)} %param.8) | copy-start | bytes 1572868
  2.3 1.0 %copy-start.2 = (f32[8,128,128]{2,1,0:T(8,128)S(1)}, f32[8,128,128]{2,1,0:T(8,128)}, u32[]{:S(2)}) copy-start(f32[8,128,128]{2,1,0:T(8,128)} %precision_hbm.1) | copy-start | bytes 1572868
  3.3 0.9 %copy-start.3 = (f32[2,128,128]{2,1,0:T(8,128)S(1)}, f32[2,128,128]{2,1,0:T(8,128)}, u32[]{:S(2)}) copy-start(f32[2,128,128]{2,1,0:T(8,128)} %map_hbm.1) | copy-start | bytes 393220
  4.2 0.7 %copy-start.4 = (s32[8,16]{1,0:T(8,128)S(1)}, s32[8,16]{1,0:T(8,128)}, u32[]{:S(2)}) copy-start(s32[8,16]{1,0:T(8,128)} %table_ref.1) | copy-start | bytes 1540
  4.9 0.7 %copy-start.5 = (s32[8]{0:T(128)S(1)}, s32[8]{0:T(128)}, u32[]{:S(2)}) copy-start(s32[8]{0:T(128)} %holder_ref.1) | copy-start | bytes 100

commit v3 on v2

--- a/solution.py
+++ b/solution.py
@@ -23,6 +23,22 @@
     both = jnp.dot(
         jnp.concatenate(split(left), axis=0), right_pair, preferred_element_type=jnp.float32)
     return both[:rows, :cols] + (both[:rows, cols:] + both[rows:, :cols])
+
+
+def split_three(value):
+    high = value.astype(jnp.bfloat16)
+    rest = value - high.astype(jnp.float32)
+    return (high,) + split(rest)
+
+
+def exact_dot(left, right_three):
+    rows, cols = left.shape[0], right_three.shape[1] // 3
+    all_pairs = jnp.dot(
+        jnp.concatenate(split_three(left), axis=0), right_three,
+        preferred_element_type=jnp.float32)
+    term = lambda i, k: all_pairs[i * rows:(i + 1) * rows, k * cols:(k + 1) * cols]
+    small = term(0, 2) + term(1, 1) + term(2, 0)
+    return term(0, 0) + ((term(0, 1) + term(1, 0)) + small)
 
 
 def exchange(
@@ -77,14 +93,14 @@
 
     loads[0].wait()
     loads[1].wait()
-    table_pair = jnp.concatenate(
-        [jnp.concatenate(split(map_ref[h]), axis=1) for h in range(layers)], axis=0)
+    map_three = jnp.concatenate(
+        [jnp.concatenate(split_three(map_ref[h]), axis=1) for h in range(layers)], axis=0)
     for b in range(blocks):
         state = jnp.concatenate([
             bg_ref[pl.ds(b * layers + h, members, stride=blocks * layers), :]
             for h in range(layers)], axis=1)
         half[b] = state.astype(jnp.bfloat16)
-        total = split_dot(state, table_pair)
+        total = exact_dot(state, map_three)
         for q in range(lev):
             part[q, b] = total[q * rows:(q + 1) * rows]
 
@@ -112,8 +128,6 @@
             copy.start()
             copies.append(copy)
 
-    early = [d for d in range(1, mem) if d in (depth, depth + 1)]
-    send_states(early)
     for c in range(CAP):
         tile, live = find(me * CAP + c)
         st_ref[me, c] = half[tile] * live.astype(jnp.bfloat16)
@@ -154,7 +168,7 @@
 
     begin(me, lv, x_send.at[0], x_recv.at[0], (side, lv))
     spread(0)
-    send_states([d for d in range(1, mem) if d not in early])
+    send_states(range(1, mem))
     pass_on(far[0], lv, x_send.at[0], x_recv.at[0], (side, lv)).wait_recv()
     spread(depth)
     for d in range(1, depth):

time: 65.4 us -> 61.3 us (0.937)
  the two profiles are of different devices: /device:TPU:0 before, /device:TPU:11 now
where the time goes in v3:
time: 61.3 us; the launch traced here: 61 us
  Pallas kernels  55.4 us (90%)
  local copies, waits for them, and re-layouts  5.55 us (9%)
    pallas_call x1, Pallas kernels, dense_shards(): pl.pallas_call(functools.partial(exchange, mem, lev), out_shape=(jax.Shap...  48 us
    pallas_call x1, Pallas kernels, dense_shards(): pl.pallas_call(analyse, out_shape=jax.ShapeDtypeStruct((mem * members * C...  7.44 us
    unnamed x12, local copies, waits for them, and re-layouts  5.55 us

profile of v3, /device:TPU:11, one launch (start us, length us, event | category | flops | bytes accessed | tf_op | source)
XLA Modules:
  0.0 61.0 jit_solution(3908388207416820488)
XLA Ops:
  0.0 0.0 copy-start
  0.0 1.2 %copy-done = f32[128,8,2,128]{3,2,1,0:T(2,128)S(1)} copy-done((f32[128,8,2,128]{3,2,1,0:T(2,128)S(1)}, f32[128,8,2,128]{3,2,1,0:T(2,128)}, u32[]{:S(2)}) %copy-start) | copy-done | bytes 1048600
  1.2 0.0 copy-start.1
  1.2 1.0 %copy-done.1 = f32[128,8,128]{2,1,0:T(8,128)S(1)} copy-done((f32[128,8,128]{2,1,0:T(8,128)S(1)}, f32[128,8,128]{2,1,0:T(8,128)}, u32[]{:S(2)}) %copy-start.1) | copy-done | bytes 524312
  2.3 0.0 copy-start.2
  2.3 1.0 %copy-done.2 = f32[8,128,128]{2,1,0:T(8,128)S(1)} copy-done((f32[8,128,128]{2,1,0:T(8,128)S(1)}, f32[8,128,128]{2,1,0:T(8,128)}, u32[]{:S(2)}) %copy-start.2) | copy-done | bytes 524312
  3.3 0.0 copy-start.3
  3.3 0.9 %copy-done.3 = f32[2,128,128]{2,1,0:T(8,128)S(1)} copy-done((f32[2,128,128]{2,1,0:T(8,128)S(1)}, f32[2,128,128]{2,1,0:T(8,128)}, u32[]{:S(2)}) %copy-start.3) | copy-done | bytes 131096
  4.2 0.0 copy-start.4
  4.2 0.7 %copy-done.4 = s32[8,16]{1,0:T(8,128)S(1)} copy-done((s32[8,16]{1,0:T(8,128)S(1)}, s32[8,16]{1,0:T(8,128)}, u32[]{:S(2)}) %copy-start.4) | copy-done | bytes 536
  4.9 0.0 copy-start.5
  4.9 0.7 %copy-done.5 = s32[8]{0:T(128)S(1)} copy-done((s32[8]{0:T(128)S(1)}, s32[8]{0:T(128)}, u32[]{:S(2)}) %copy-start.5) | copy-done | bytes 56
  5.6 48.0 %exchange.1 = (bf16[8,4,2,8,32,128]{5,4,3,2,1,0:T(8,128)(2,1)S(1)}, bf16[8,2,128,256]{3,2,1,0:T(8,128)(2,1)S(1)}, f32[16]{0:T(128)S(1)}) custom-call(s32[8]{0:T(128)S(1)} %copy-done.5, s32[8,16]{1,0:T(8,128)S(1)} %copy-done.4, f32[2048,128]{1,0:T(8,128)S(1)} %bitcast.3, f32[2,128,128]{2,1,0:T(8,128)S(1)} %copy-done.3, f32[1024,128]{1,0:T(8,128)S(1)} %bitcast.4, ...), custom_call_target="tpu_custom_call" | custom-call | tf_op jit(solution)/shard_map/exchange/pallas_call | solution.py:260
  53.5 7.4 %analyse.1 = f32[4096,128]{1,0:T(8,128)} custom-call(f32[16]{0:T(128)S(1)} %get-tuple-element.8.scale_ref, bf16[8,4,2,8,32,128]{5,4,3,2,1,0:T(8,128)(2,1)S(1)} %get-tuple-element.9.pw_ref, bf16[8,2,128,256]{3,2,1,0:T(8,128)(2,1)S(1)} %get-tuple-element.10.st_ref), custom_call_target="tpu_custom_call" | custom-call | tf_op jit(solution)/shard_map/analyse/pallas_call | solution.py:291
Async XLA Ops:
  0.0 1.2 %copy-start = (f32[128,8,2,128]{3,2,1,0:T(2,128)S(1)}, f32[128,8,2,128]{3,2,1,0:T(2,128)}, u32[]{:S(2)}) copy-start(f32[128,8,2,128]{3,2,1,0:T(2,128)} %param.6) | copy-start | bytes 3145732
  1.2 1.0 %copy-start.1 = (f32[128,8,128]{2,1,0:T(8,128)S(1)}, f32[128,8,128]{2,1,0:T(8,128)}, u32[]{:S(2)}) copy-start(f32[128,8,128]{2,1,0:T(8,128)} %param.8) | copy-start | bytes 1572868
  2.3 1.0 %copy-start.2 = (f32[8,128,128]{2,1,0:T(8,128)S(1)}, f32[8,128,128]{2,1,0:T(8,128)}, u32[]{:S(2)}) copy-start(f32[8,128,128]{2,1,0:T(8,128)} %precision_hbm.1) | copy-start | bytes 1572868
  3.3 0.9 %copy-start.3 = (f32[2,128,128]{2,1,0:T(8,128)S(1)}, f32[2,128,128]{2,1,0:T(8,128)}, u32[]{:S(2)}) copy-start(f32[2,128,128]{2,1,0:T(8,128)} %map_hbm.1) | copy-start | bytes 393220
  4.2 0.7 %copy-start.4 = (s32[8,16]{1,0:T(8,128)S(1)}, s32[8,16]{1,0:T(8,128)}, u32[]{:S(2)}) copy-start(s32[8,16]{1,0:T(8,128)} %table_ref.1) | copy-start | bytes 1540
  4.9 0.7 %copy-start.5 = (s32[8]{0:T(128)S(1)}, s32[8]{0:T(128)}, u32[]{:S(2)}) copy-start(s32[8]{0:T(128)} %holder_ref.1) | copy-start | bytes 100

commit v4 on v3

--- a/solution.py
+++ b/solution.py
@@ -44,7 +44,8 @@
 def exchange(
     mem, lev,
     holder_ref, table_ref, bg_hbm, map_hbm, sensed_hbm, precision_hbm,
-    pw_ref, st_ref, scale_ref,
+    out_hbm,
+    pw_ref, st_ref, scale_ref, out_ref, covariance, out_sem,
     bg_ref, map_ref, sensed_ref, precision_ref, local_sem,
     half, outgoing, part, arrived, pairs,
     part_send, part_recv, state_send, state_recv, z_send, z_recv, x_send, x_recv,
@@ -204,11 +205,12 @@
         pltpu.make_async_remote_copy(
             outgoing.at[d], st_ref.at[source], state_send.at[d], state_recv.at[d],
             device_id=(source, lv), device_id_type=MESH).wait_recv()
+    analyse(scale_ref, pw_ref, st_ref, out_ref, out_hbm, covariance, out_sem)
     for c in part_copies + copies:
         c.wait_send()
 
 
-def analyse(scale_ref, pw_ref, st_ref, out_ref, covariance):
+def analyse(scale_ref, pw_ref, st_ref, out_ref, out_hbm, covariance, out_sem):
     mem, lev, _, blocks, rows, obs = pw_ref.shape
     capacity, members, width = st_ref.shape[1:]
     total = mem * members
@@ -225,25 +227,30 @@
             covariance[pl.ds(pl.multiple_of(b * obs, obs), obs), c * width:(c + 1) * width] = (
                 cov * scale_ref[c * blocks + b]).astype(jnp.bfloat16)
 
-    parts = 4 if mem % 4 == 0 else mem
+    parts = 2
     chunk = mem // parts
-
-    @pl.loop(0, parts)
-    def _(r):
+    stores = []
+    for r in range(parts):
         owners = pl.ds(r * chunk, chunk)
         weighted = jnp.concatenate(
             [pw_ref[owners, :, 1, b].reshape(chunk * members, obs) for b in range(blocks)], axis=1)
         per_slot = width // 128
+        stride = capacity * per_slot
         for c in range(capacity):
             rise = jnp.dot(
                 weighted, covariance[:, c * width:(c + 1) * width],
                 preferred_element_type=jnp.float32)
             value = st_ref[owners, c].reshape(chunk * members, width).astype(jnp.float32) + rise
             for h in range(per_slot):
-                stride = capacity * per_slot
                 start = r * chunk * members * stride + c * per_slot + h
                 out_ref[pl.ds(start, chunk * members, stride=stride), :] = (
                     value[:, h * 128:(h + 1) * 128])
+        whole = pl.ds(r * chunk * members * stride, chunk * members * stride)
+        store = pltpu.make_async_copy(out_ref.at[whole], out_hbm.at[whole], out_sem.at[r])
+        store.start()
+        stores.append(store)
+    for store in stores:
+        store.wait()
 
 
 def dense_shards(mem, lev, bg, linear_map, sensed, precision, table, holder_rank):
@@ -252,21 +259,22 @@
     rows = members // lev
     width = layers * sites
     smem = pl.BlockSpec(memory_space=pltpu.SMEM)
-    vmem = pl.BlockSpec(memory_space=pltpu.VMEM)
     hbm = pl.BlockSpec(memory_space=pltpu.HBM)
     dma = pltpu.SemaphoreType.DMA
     half = jnp.bfloat16
     wide = jnp.float32
-    pw, st, scale = pl.pallas_call(
+    out = pl.pallas_call(
         functools.partial(exchange, mem, lev),
-        out_shape=(
-            jax.ShapeDtypeStruct((mem, lev, 2, blocks, rows, obs), half),
-            jax.ShapeDtypeStruct((mem, CAP, members, width), half),
-            jax.ShapeDtypeStruct((CAP * blocks,), wide),
-        ),
+        out_shape=jax.ShapeDtypeStruct((mem * members * CAP * layers, sites), wide),
         in_specs=[smem, smem, hbm, hbm, hbm, hbm],
-        out_specs=(vmem, vmem, smem),
+        out_specs=hbm,
         scratch_shapes=[
+            pltpu.VMEM((mem, lev, 2, blocks, rows, obs), half),
+            pltpu.VMEM((mem, CAP, members, width), half),
+            pltpu.SMEM((CAP * blocks,), wide),
+            pltpu.VMEM((mem * members * CAP * layers, sites), wide),
+            pltpu.VMEM((blocks * obs, CAP * width), half),
+            dma((2,)),
             pltpu.VMEM((members * blocks * layers, sites), wide),
             pltpu.VMEM(linear_map.shape, wide),
             pltpu.VMEM((members * blocks, obs), wide),
@@ -282,21 +290,12 @@
             dma((mem,)), dma((mem,)), dma((2, mem)), dma((2, mem)),
         ],
         compiler_params=pltpu.CompilerParams(
-            collective_id=0, has_side_effects=True, vmem_limit_bytes=40 * 2**20),
+            collective_id=0, has_side_effects=True, vmem_limit_bytes=60 * 2**20),
         name="exchange",
     )(
         holder_rank, table, bg.reshape(members * blocks * layers, sites), linear_map,
         sensed.reshape(members * blocks, obs), precision,
     )
-    out = pl.pallas_call(
-        analyse,
-        out_shape=jax.ShapeDtypeStruct((mem * members * CAP * layers, sites), jnp.float32),
-        in_specs=[smem, vmem, vmem],
-        out_specs=vmem,
-        scratch_shapes=[pltpu.VMEM((blocks * obs, CAP * width), half)],
-        compiler_params=pltpu.CompilerParams(vmem_limit_bytes=40 * 2**20),
-        name="analyse",
-    )(scale, pw, st)
     return out.reshape(mem * members, CAP, layers, sites)
 
 

time: 61.3 us -> 57.2 us (0.933)
  Pallas kernels: 55.4 us -> 53.4 us
  local copies, waits for them, and re-layouts: 5.55 us -> 3.63 us
    pallas_call x2 -> x1, Pallas kernels: 55.4 us -> 53.4 us  [dense_shards(): pl.pallas_call(functools.partial(exchange, mem, lev), out_shape=jax.Shape...]
    unnamed x12 -> x1, local copies, waits for them, and re-layouts: 5.55 us -> 3.63 us
where the time goes in v4:
time: 57.2 us; the launch traced here: 57 us
  Pallas kernels  53.4 us (93%)
  local copies, waits for them, and re-layouts  3.63 us (6%)
    pallas_call x1, Pallas kernels, dense_shards(): pl.pallas_call(functools.partial(exchange, mem, lev), out_shape=jax.Shape...  53.4 us
    unnamed x1, local copies, waits for them, and re-layouts  3.63 us

profile of v4, /device:TPU:11, one launch (start us, length us, event | category | flops | bytes accessed | tf_op | source)
XLA Modules:
  0.0 57.0 jit_solution(15899492443564856594)
XLA Ops:
  0.0 53.4 %exchange.1 = f32[4096,128]{1,0:T(8,128)} custom-call(s32[8]{0:T(128)} %holder_ref.1, s32[8,16]{1,0:T(8,128)} %table_ref.1, f32[2048,128]{1,0:T(8,128)} %bitcast.4, f32[2,128,128]{2,1,0:T(8,128)} %map_hbm.1, f32[1024,128]{1,0:T(8,128)} %bitcast.5, f32[8,128,128]{2,1,0:T(8,128)} %precision_hbm.1), custom_call_target="tpu_custom_call" | custom-call | tf_op jit(solution)/shard_map/exchange/pallas_call | solution.py:266
  53.4 3.6 %copy.8 = f32[1024,2,2,128]{3,2,1,0:T(2,128)} copy(f32[1024,2,2,128]{3,2,1,0:T(2,128)} %bitcast.3) | data formatting | bytes 4194304
